TPU v7x, 32 devices: a whole 2x2x4 slice. The times are simulated.
32 devices in a mesh: groups: 2 (over x), ctx: 16 (over z, y, core).
Axes of the slice: x: 2, y: 2, z: 4, core: 2. Of those that a mesh axis runs over, the one named last changes fastest.
Arguments:
- hidden: bfloat16 [4096, 4096], P(('groups', 'ctx')), parts along dimension 0, may hold values from -6 to 6
- queries: bfloat16 [4096, 4096], P(('groups', 'ctx')), parts along dimension 0, may hold values from -64 to 64
- cache_weight: bfloat16 [4096, 1024], P('ctx'), may hold values from -0.09375 to 0.09375
- pattern: int32 [32, 7], P('groups'), parts along dimension 0, may hold values from -1 to 15, as said below
- span_pairs: int32 [32], P('groups'), parts along dimension 0, may hold values from 0 to 15, each once
Outputs:
- attended: bfloat16 [4096, 4096], P(('groups', 'ctx')), parts along dimension 0
There are 2 independent parts, one for each index of `groups`. A program takes and returns all parts, laid end to end along the dimension named above; an argument that names none is the same for every part. Nothing has to cross between parts.
Inputs may be any that keep to these rules, and one draw needn't show every extreme that they name: `pattern`: row b lists b, b - 1, and so on down to max(0, b - 3), then, in rising order, the blocks below b - 3 that leave the same remainder, drawn for the row, modulo 4; the remaining entries are -1. `span_pairs`: A permutation.
All inputs are finite; a program needn't handle non-finite values.
Results may differ from a plain program's by a relative error of at most 0.004.
The roundings to bfloat16 on the way count: a program that leaves them out, or rounds other values in their place, can miss the bound.
Values may be sent and summed in bfloat16 or wider, within the bound.
A program may use at most 192 MiB of HBM per device.

v0:
```python
import jax
import jax.numpy as jnp
from jax import lax
from jax.sharding import PartitionSpec as P

QH = 32
KVH = 4
HD = 128
BLOCK = 128


ROPE_BASE = 500000.0
MASKED = -1e30


def rotary(values, positions, head_count, head_size):
    half_size = head_size // 2
    frequency = ROPE_BASE ** (-(jnp.arange(half_size, dtype=jnp.float32) * 2.0 / head_size))
    angles = positions.astype(jnp.float32)[:, None] * frequency[None, :]
    cosine = jnp.cos(angles)[:, None, :]
    sine_part = jnp.sin(angles)[:, None, :]
    shaped = values.reshape(values.shape[0], head_count, head_size)
    front_part = shaped[..., :half_size]
    back_part = shaped[..., half_size:]
    turned = jnp.concatenate(
        [front_part * cosine - back_part * sine_part, back_part * cosine + front_part * sine_part],
        axis=-1,
    )
    return turned.reshape(values.shape[0], head_count * head_size)


def body(hidden, queries, cache_weight, pattern, span_pairs):
    tok_rows = hidden.shape[0]
    device_count = lax.axis_size("ctx")
    device_index = lax.axis_index("ctx")
    span_size = tok_rows // 2
    unit_size = BLOCK // 2
    group_size = QH // KVH
    cache_width = KVH * HD
    score_scale = HD ** (-0.5)
    low_span = span_pairs[device_index]
    high_span = 2 * device_count - 1 - low_span
    offsets = jnp.arange(span_size, dtype=jnp.int32)
    positions = jnp.concatenate([low_span * span_size + offsets, high_span * span_size + offsets])
    projected = jnp.dot(
        hidden,
        lax.all_gather(cache_weight, "ctx", axis=0, tiled=True),
        preferred_element_type=jnp.float32,
    )
    key_local = rotary(projected[:, :cache_width], positions, KVH, HD).astype(jnp.bfloat16)
    value_local = projected[:, cache_width:].astype(jnp.bfloat16)
    key_table, value_table = (
        lax.all_gather(key_local, "ctx", axis=0, tiled=True),
        lax.all_gather(value_local, "ctx", axis=0, tiled=True),
    )
    rotated = rotary(queries.astype(jnp.float32), positions, QH, HD).astype(jnp.bfloat16)
    pair_ids = jnp.arange(device_count, dtype=jnp.int32)
    owners = jnp.sum(
        jnp.where(span_pairs[None, :] == pair_ids[:, None], pair_ids[None, :], 0), axis=1
    )
    units_per_span = span_size // unit_size

    def unit_row(unit_id):
        span_id = unit_id // units_per_span
        within = unit_id % units_per_span
        upper_half = span_id >= device_count
        owner_span = jnp.where(upper_half, 2 * device_count - 1 - span_id, span_id)
        owner_device = owners[owner_span]
        return owner_device * tok_rows + jnp.where(upper_half, span_size, 0) + within * unit_size

    def fetch_block(block_id):
        block_safe = jnp.maximum(block_id, 0)
        first_row = unit_row(2 * block_safe)
        second_row = unit_row(2 * block_safe + 1)
        key_part = jnp.concatenate(
            [
                lax.dynamic_slice_in_dim(key_table, first_row, unit_size, 0),
                lax.dynamic_slice_in_dim(key_table, second_row, unit_size, 0),
            ],
            axis=0,
        )
        value_part = jnp.concatenate(
            [
                lax.dynamic_slice_in_dim(value_table, first_row, unit_size, 0),
                lax.dynamic_slice_in_dim(value_table, second_row, unit_size, 0),
            ],
            axis=0,
        )
        key_pos = block_safe * BLOCK + jnp.arange(BLOCK, dtype=jnp.int32)
        key_live = jnp.broadcast_to(block_id >= 0, (BLOCK,))
        return (key_part, value_part, key_pos, key_live)

    slot_count = pattern.shape[1]
    block_lists = jnp.concatenate([pattern, jnp.full((pattern.shape[0], 1), -1, jnp.int32)], axis=1)
    group_count = (slot_count + 1) // 2
    unit_count = tok_rows // unit_size

    def attend_unit(unit_index):
        row_start = unit_index * unit_size
        query_pos = lax.dynamic_slice_in_dim(positions, row_start, unit_size, 0)
        query_block = query_pos[0] // BLOCK
        query_rows = lax.dynamic_slice_in_dim(rotated, row_start, unit_size, 0)
        query_heads = query_rows.reshape(unit_size, KVH, group_size, HD)
        block_list = lax.dynamic_index_in_dim(block_lists, query_block, 0, keepdims=False)

        def fill_turn(turn_index, buffers):
            score_store, value_store = buffers
            key_one, value_one, pos_one, live_one = fetch_block(block_list[2 * turn_index])
            key_two, value_two, pos_two, live_two = fetch_block(block_list[2 * turn_index + 1])
            key_part = jnp.concatenate([key_one, key_two], axis=0).reshape(2 * BLOCK, KVH, HD)
            value_part = jnp.concatenate([value_one, value_two], axis=0).reshape(2 * BLOCK, KVH, HD)
            key_pos = jnp.concatenate([pos_one, pos_two])
            key_live = jnp.concatenate([live_one, live_two])
            scores = (
                jnp.einsum(
                    "qhgd,khd->qhgk", query_heads, key_part, preferred_element_type=jnp.float32
                )
                * score_scale
            )
            allowed = key_live[None, :] & (key_pos[None, :] <= query_pos[:, None])
            masked = jnp.where(allowed[:, None, None, :], scores, MASKED)
            score_store = lax.dynamic_update_index_in_dim(score_store, masked, turn_index, 0)
            value_store = lax.dynamic_update_index_in_dim(value_store, value_part, turn_index, 0)
            return (score_store, value_store)

        start_scores = jnp.full(
            (group_count, unit_size, KVH, group_size, 2 * BLOCK), MASKED, jnp.float32
        )
        start_values = jnp.zeros((group_count, 2 * BLOCK, KVH, HD), jnp.bfloat16)
        score_store, value_store = lax.fori_loop(
            0, group_count, fill_turn, (start_scores, start_values)
        )
        row_peak = jnp.max(score_store, axis=(0, 4))
        alive = score_store > 0.5 * MASKED
        weights = jnp.where(alive, jnp.exp(score_store - row_peak[None, ..., None]), 0.0).astype(
            jnp.bfloat16
        )
        totals = jnp.sum(weights.astype(jnp.float32), axis=(0, 4))
        weighted = jnp.einsum(
            "tqhgk,tkhd->qhgd", weights, value_store, preferred_element_type=jnp.float32
        )
        return (weighted / totals[..., None]).reshape(unit_size, QH * HD).astype(jnp.bfloat16)

    attended = lax.map(attend_unit, jnp.arange(unit_count, dtype=jnp.int32))
    return attended.reshape(tok_rows, QH * HD)


def solution(mesh):
    in_specs = (
        P(("groups", "ctx"), None),
        P(("groups", "ctx"), None),
        P("ctx", None),
        P("groups", None),
        P("groups"),
    )
    out_specs = P(("groups", "ctx"), None)
    return jax.shard_map(body, mesh=mesh, in_specs=in_specs, out_specs=out_specs, check_vma=False)
```

profile of v0, /device:TPU:1, one launch (start us, length us, event | category | flops | bytes accessed | tf_op | source)
XLA Modules:
  0.0 303.7 jit_solution(8553468144738225183)
XLA Ops:
  7.3 1.2 dynamic_slice.173
  10.3 76.7 %all-gather.4.cloned.1.call-done = bf16[4096,1024]{1,0:T(8,128)(2,1)} async-done(((bf16[256,1024]{1,0:T(8,128)(2,1)}), bf16[4096,1024]{1,0:T(8,128)(2,1)}) %all-gather.4.cloned.1.call-update) | async-done | bytes 8388624 | tf_op jit(solution)/shard_map/all_gather | solution.py:47
  87.0 4.6 %fusion.14 = f32[128,1024]{1,0:T(8,128)S(1)} fusion(bf16[128,4096]{1,0:T(8,128)(2,1)S(1)} %copy-done, bf16[4096,1024]{1,0:T(8,128)(2,1)} %all-gather.4.cloned.1.call-done), kind=kOutput, calls=%fused_computation.48 | convolution fusion | flops 1073741824 | bytes 9961472 | tf_op jit(solution)/shard_map/dot_general | solution.py:45
  96.5 36.2 %all-gather.6.cloned.1.call-done = bf16[2048,512]{0,1:T(8,128)(2,1)} async-done(((bf16[128,512]{0,1:T(8,128)(2,1)}), bf16[2048,512]{0,1:T(8,128)(2,1)}) %all-gather.6.cloned.1.call-update) | async-done | bytes 2097168 | tf_op jit(solution)/shard_map/all_gather | solution.py:53
  132.6 42.5 %all-gather.8.cloned.1.call-done = bf16[2048,512]{1,0:T(8,128)(2,1)} async-done(((bf16[128,512]{1,0:T(8,128)(2,1)}), bf16[2048,512]{1,0:T(8,128)(2,1)}) %all-gather.8.cloned.1.call-update) | async-done | bytes 2097168 | tf_op jit(solution)/shard_map/all_gather | solution.py:54
  175.2 122.0 %while.44 = (s32[]{:T(128)}, bf16[2,64,4096]{2,1,0:T(8,128)(2,1)}, s32[2]{0:T(128)S(1)}, s32[128]{0:T(128)S(1)}, s32[16,8]{1,0:T(8,128)S(1)}, /*index=5*/bf16[12...) while((s32[]{:T(128)}, bf16[2,64,4096]{2,1,0:T(8,128)(2,1)}, ...), condition=%wide.region_6.7_spmd, body=%wide.region_1.6_spmd.sunk | while | flops 689467968 | bytes 43328316 | solution.py:144
  177.2 47.9 %while.45 = (s32[]{:T(128)}, f32[4,64,4,8,256]{4,1,3,2,0:T(8,128)}, bf16[4,256,4,128]{3,2,1,0:T(4,128)(2,1)}, s32[8]{0:T(128)S(1)}, s32[64]{0:T(128)S(1)}, /*ind...) while((s32[]{:T(128)}, f32[4,64,4,8,256]{4,1,3,2,0:T(8,128)}, ...), condition=%wide.region_3.3_spmd, body=%wide.region_2.2_spmd.sunk | while | flops 137396800 | bytes 6069289 | solution.py:130
  182.5 1.3 constant_dynamic-slice_fusion.11
  185.5 1.8 bitcast_dynamic-update-slice_fusion.2
  187.3 1.0 constant_dynamic-slice_fusion.12
  194.5 1.3 constant_dynamic-slice_fusion.11
  197.5 1.7 bitcast_dynamic-update-slice_fusion.2
  199.2 1.0 constant_dynamic-slice_fusion.12
  206.4 1.3 constant_dynamic-slice_fusion.11
  209.4 1.8 bitcast_dynamic-update-slice_fusion.2
  218.4 1.3 constant_dynamic-slice_fusion.11
  221.4 1.8 bitcast_dynamic-update-slice_fusion.2
  225.0 3.8 %reduce_max.14 = f32[64,4,8]{0,2,1:T(8,128)S(1)} reduce(f32[4,64,4,8,256]{4,1,3,2,0:T(8,128)} %get-tuple-element.658, f32[]{:T(128)} %constant.381.clone.1..sunk), dimensions={0,4}, to_apply=%region_4.4 | reduce | flops 2095104 | bytes 8396804 | tf_op jit(solution)/shard_map/while/body/eval_jaxpr/reduce_max | solution.py:133
  228.9 4.6 %convert_reduce_fusion.2 = (f32[64,4,8]{0,2,1:T(8,128)S(1)}, bf16[4,64,4,8,256]{4,1,3,2,0:T(8,128)(2,1)S(1)}) fusion(f32[4,64,4,8,256]{4,1,3,2,0:T(8,128)} %get-tuple-element.658, f32[64,4,8]{0,2,1:T(8,128)S(1)} %reduce_max.14), kind=kLoop, calls=%fused_computation.17.clone.1 | loop fusion | flops 12580864 | bytes 12599296 | tf_op jit(solution)/shard_map/while/body/eval_jaxpr/reduce_sum | solution.py:138
  233.5 1.2 divide_convert_fusion.2
  238.2 47.9 %while.45 = (s32[]{:T(128)}, f32[4,64,4,8,256]{4,1,3,2,0:T(8,128)}, bf16[4,256,4,128]{3,2,1,0:T(4,128)(2,1)}, s32[8]{0:T(128)S(1)}, s32[64]{0:T(128)S(1)}, /*ind...) while((s32[]{:T(128)}, f32[4,64,4,8,256]{4,1,3,2,0:T(8,128)}, ...), condition=%wide.region_3.3_spmd, body=%wide.region_2.2_spmd.sunk | while | flops 137396800 | bytes 6069289 | solution.py:130
  243.5 1.3 constant_dynamic-slice_fusion.11
  246.5 1.8 bitcast_dynamic-update-slice_fusion.2
  255.5 1.3 constant_dynamic-slice_fusion.11
  258.5 1.7 bitcast_dynamic-update-slice_fusion.2
  267.4 1.3 constant_dynamic-slice_fusion.11
  270.4 1.8 bitcast_dynamic-update-slice_fusion.2
  279.4 1.3 constant_dynamic-slice_fusion.11
  282.4 1.8 bitcast_dynamic-update-slice_fusion.2
  286.0 3.8 %reduce_max.14 = f32[64,4,8]{0,2,1:T(8,128)S(1)} reduce(f32[4,64,4,8,256]{4,1,3,2,0:T(8,128)} %get-tuple-element.658, f32[]{:T(128)} %constant.381.clone.1..sunk), dimensions={0,4}, to_apply=%region_4.4 | reduce | flops 2095104 | bytes 8396804 | tf_op jit(solution)/shard_map/while/body/eval_jaxpr/reduce_max | solution.py:133
  289.9 4.6 %convert_reduce_fusion.2 = (f32[64,4,8]{0,2,1:T(8,128)S(1)}, bf16[4,64,4,8,256]{4,1,3,2,0:T(8,128)(2,1)S(1)}) fusion(f32[4,64,4,8,256]{4,1,3,2,0:T(8,128)} %get-tuple-element.658, f32[64,4,8]{0,2,1:T(8,128)S(1)} %reduce_max.14), kind=kLoop, calls=%fused_computation.17.clone.1 | loop fusion | flops 12580864 | bytes 12599296 | tf_op jit(solution)/shard_map/while/body/eval_jaxpr/reduce_sum | solution.py:138
  294.5 1.2 divide_convert_fusion.2
  (154 shorter events, 36.8 us)
Async XLA Ops:
  6.5 80.4 %copy-start = (bf16[128,4096]{1,0:T(8,128)(2,1)S(1)}, bf16[128,4096]{1,0:T(8,128)(2,1)}, u32[]{:S(2)}) copy-start(bf16[128,4096]{1,0:T(8,128)(2,1)} %param.9) | copy-start | bytes 3145732
  6.5 80.4 %all-gather.4.cloned.1.call-start = ((), (), s32[]{:S(2)}) async-start(), calls=%async_computation | async-start | bytes 8912896 | tf_op jit(solution)/shard_map/all_gather | solution.py:47
  7.3 125.4 %all-gather.6.cloned.1.call-start = ((), (), s32[]{:S(2)}) async-start(), calls=%async_computation.1 | async-start | bytes 2228224 | tf_op jit(solution)/shard_map/all_gather | solution.py:53
  91.6 2.2 copy-start.1
  93.0 82.1 %all-gather.8.cloned.1.call-start = ((), (), s32[]{:S(2)}) async-start(), calls=%async_computation.2 | async-start | bytes 2228224 | tf_op jit(solution)/shard_map/all_gather | solution.py:54
  95.2 1.1 copy-start.2
  95.2 1.2 copy-start.4
  228.9 4.6 %copy-start.3 = (bf16[4,256,4,128]{3,2,1,0:T(4,128)(2,1)S(1)}, bf16[4,256,4,128]{3,2,1,0:T(4,128)(2,1)}, u32[]{:S(2)}) copy-start(bf16[4,256,4,128]{3,2,1,0:T(4,128)(2,1)} %get-tuple-element.659) | copy-start | bytes 3145732 | tf_op jit(solution)/shard_map/while
  289.9 4.6 %copy-start.3 = (bf16[4,256,4,128]{3,2,1,0:T(4,128)(2,1)S(1)}, bf16[4,256,4,128]{3,2,1,0:T(4,128)(2,1)}, u32[]{:S(2)}) copy-start(bf16[4,256,4,128]{3,2,1,0:T(4,128)(2,1)} %get-tuple-element.659) | copy-start | bytes 3145732 | tf_op jit(solution)/shard_map/while
Sparse Core Ops, SparseCore 0:
  9.5 77.3 all-gather.3
  93.2 39.4 all-gather.5
  134.8 40.3 all-gather.7
where the time goes:
time: 305 us; the launch traced here: 304 us
  waiting for transfers between devices  156 us (51%)
  loops' own time  45 us (15%)
  local copies, waits for them, and re-layouts  44.8 us (15%)
  other arithmetic  21.9 us (7%)
  matrix products  21.3 us (7%)
  between operations  14.6 us (5%)
    all_gather x1, waiting for transfers between devices, body(): lax.all_gather(cache_weight, 'ctx', axis=0, tiled=True)  76.7 us
    another operation x2, loops' own time, attend_unit(): lax.fori_loop(0, group_count, fill_turn, (start_scores, start_values))  43.1 us
    all_gather x1, waiting for transfers between devices, body(): lax.all_gather(value_local, 'ctx', axis=0, tiled=True)  42.5 us
    all_gather x1, waiting for transfers between devices, body(): lax.all_gather(key_local, 'ctx', axis=0, tiled=True)  36.2 us
    dot_general x8, matrix products, fill_turn(): jnp.einsum('qhgd,khd->qhgk', query_heads, key_part, preferred_element_typ...  14.2 us
    dynamic_slice x8, local copies, waits for them, and re-layouts, fetch_block(): lax.dynamic_slice_in_dim(key_table, first_row, unit_size, 0)  10.6 us
    reduce_sum x2, other arithmetic, attend_unit(): totals = jnp.sum(weights.astype(jnp.float32), axis=(0, 4))  9.22 us
    reduce_max x2, other arithmetic, attend_unit(): row_peak = jnp.max(score_store, axis=(0, 4))  7.66 us
  transfers between devices with their start and end apart: 3, of which 3 were waited for; matrix products, arithmetic and copies ran while one was open for 2% of the time, Pallas kernels for 0%

commit v1 on v0

v1 whole, which is shorter than its diff:
```python
import functools
import math

import jax
import jax.numpy as jnp
from jax import lax
from jax.experimental import pallas as pl
from jax.experimental.pallas import tpu as pltpu
from jax.sharding import PartitionSpec as P

QH = 32
KVH = 4
HD = 128
BLOCK = 128
ROPE_BASE = 500000.0
MASKED = -1e30
CHUNK = 2 * BLOCK


def rope_tables(positions):
    half = HD // 2
    frequency = ROPE_BASE ** (-(jnp.arange(half, dtype=jnp.float32) * 2.0 / HD))
    angles = positions.astype(jnp.float32)[:, None] * frequency[None, :]
    cosine, sine = jnp.cos(angles), jnp.sin(angles)
    return (
        jnp.concatenate([cosine, cosine], axis=1),
        jnp.concatenate([-sine, sine], axis=1),
    )


def attend_kernel(
    n, pattern_ref, spans_ref, rot_ref, kv_ref, out_ref, kbuf, vbuf, scores, owner
):
    me = lax.axis_index("ctx")
    tok_rows = out_ref.shape[0]
    span = tok_rows // 2
    width = kv_ref.shape[2]
    group = QH // KVH
    rows = group * span
    slots = pattern_ref.shape[1]
    factor = HD ** (-0.5) * math.log2(math.e)

    def place(d, carry):
        owner[spans_ref[d]] = d
        return carry

    lax.fori_loop(0, n, place, 0)
    vbuf[:, :, HD:] = jnp.ones_like(vbuf[:, :, HD:])
    low = spans_ref[me]

    for part in range(2):
        span_id = low if part == 0 else 2 * n - 1 - low
        query_block = span_id * span // BLOCK
        offset = span_id * span - query_block * BLOCK

        def fill(i, count):
            block = pattern_ref[query_block, i]

            @pl.when(block >= 0)
            def _():
                for e in range(2):
                    unit = 2 * block + e
                    upper = unit >= n
                    device = owner[jnp.where(upper, 2 * n - 1 - unit, unit)]
                    row = pl.multiple_of(device * tok_rows + jnp.where(upper, span, 0), span)
                    to = pl.ds(pl.multiple_of(count * BLOCK + e * span, span), span)
                    for h in range(KVH):
                        for buf, col in ((kbuf, h * HD), (vbuf, (KVH + h) * HD)):
                            buf[h, to, :HD] = kv_ref[
                                col // width, pl.ds(row, span), col % width : col % width + HD
                            ]

            return count + (block >= 0).astype(jnp.int32)

        count = lax.fori_loop(0, slots, fill, jnp.int32(0))

        @pl.when(count % 2 == 1)
        def _():
            to = pl.ds(pl.multiple_of(count * BLOCK, BLOCK), BLOCK)
            kbuf[:, to, :] = jnp.zeros((KVH, BLOCK, HD), kbuf.dtype)
            vbuf[:, to, :HD] = jnp.zeros((KVH, BLOCK, HD), vbuf.dtype)

        chunks = (count + 1) // 2

        for h in range(KVH):
            query = rot_ref[part, h * group : (h + 1) * group].reshape(rows, HD)

            def score(c, peak):
                keys = kbuf[h, pl.ds(pl.multiple_of(c * CHUNK, CHUNK), CHUNK), :]
                s = lax.dot_general(
                    query, keys, (((1,), (1,)), ((), ())), preferred_element_type=jnp.float32
                )
                col = c * CHUNK + lax.broadcasted_iota(jnp.int32, (span, CHUNK), 1)
                line = offset + lax.broadcasted_iota(jnp.int32, (span, CHUNK), 0)
                live = (col < count * BLOCK) & ((col >= BLOCK) | (col <= line))
                bias = jnp.where(live, 0.0, MASKED)
                s = (s.reshape(group, span, CHUNK) + bias[None]).reshape(rows, CHUNK)
                scores[c] = s
                return jnp.maximum(peak, jnp.maximum(s[:, :BLOCK], s[:, BLOCK:]))

            peak = lax.fori_loop(
                0, chunks, score, jnp.full((rows, BLOCK), MASKED, jnp.float32)
            )
            top = jnp.max(peak, axis=1, keepdims=True)

            def mix(c, total):
                weights = jnp.exp2((scores[c] - top) * factor).astype(jnp.bfloat16)
                values = vbuf[h, pl.ds(pl.multiple_of(c * CHUNK, CHUNK), CHUNK), :]
                return total + jnp.dot(weights, values, preferred_element_type=jnp.float32)

            total = lax.fori_loop(0, chunks, mix, jnp.zeros((rows, 2 * HD), jnp.float32))
            result = (total[:, :HD] / total[:, HD:]).astype(jnp.bfloat16)
            for j in range(group):
                head = h * group + j
                out_ref[part * span : (part + 1) * span, head * HD : (head + 1) * HD] = result[
                    j * span : (j + 1) * span
                ]


def attend(n, pattern, span_pairs, rotated, kv, tok_rows):
    span = tok_rows // 2
    chunks = (pattern.shape[1] + 1) // 2
    keys = chunks * CHUNK
    rows = QH // KVH * span
    smem = pl.BlockSpec(memory_space=pltpu.SMEM)
    vmem = pl.BlockSpec(memory_space=pltpu.VMEM)
    return pl.pallas_call(
        functools.partial(attend_kernel, n),
        out_shape=jax.ShapeDtypeStruct((tok_rows, QH * HD), jnp.bfloat16),
        in_specs=[smem, smem, vmem, vmem],
        out_specs=vmem,
        scratch_shapes=[
            pltpu.VMEM((KVH, keys, HD), jnp.bfloat16),
            pltpu.VMEM((KVH, keys, 2 * HD), jnp.bfloat16),
            pltpu.VMEM((chunks, rows, CHUNK), jnp.float32),
            pltpu.SMEM((n,), jnp.int32),
        ],
        compiler_params=pltpu.CompilerParams(vmem_limit_bytes=52 * 1024 * 1024),
    )(pattern, span_pairs, rotated, kv)


def body(hidden, queries, cache_weight, pattern, span_pairs):
    tok_rows = hidden.shape[0]
    n = lax.axis_size("ctx")
    me = lax.axis_index("ctx")
    span = tok_rows // 2
    low = span_pairs[me]
    offsets = jnp.arange(span, dtype=jnp.int32)
    positions = jnp.concatenate([low * span + offsets, (2 * n - 1 - low) * span + offsets])
    cosine, sine = rope_tables(positions)

    def turn(x, heads):
        x = x.reshape(tok_rows, heads, HD)
        swapped = jnp.concatenate([x[..., HD // 2 :], x[..., : HD // 2]], axis=-1)
        return x * cosine[:, None] + swapped * sine[:, None]

    projected = jnp.dot(
        hidden,
        lax.all_gather(cache_weight, "ctx", axis=0, tiled=True),
        preferred_element_type=jnp.float32,
    )
    keys = turn(projected[:, : KVH * HD], KVH).reshape(tok_rows, KVH * HD)
    local = jnp.concatenate([keys, projected[:, KVH * HD :]], axis=1).astype(jnp.bfloat16)
    kv = lax.all_gather(local, "ctx", axis=0, tiled=True)[None]
    rotated = turn(queries.astype(jnp.float32), QH).astype(jnp.bfloat16)
    rotated = rotated.reshape(2, span, QH, HD).transpose(0, 2, 1, 3)
    return attend(n, pattern, span_pairs, rotated, kv, tok_rows)


def solution(mesh):
    in_specs = (
        P(("groups", "ctx"), None),
        P(("groups", "ctx"), None),
        P("ctx", None),
        P("groups", None),
        P("groups"),
    )
    return jax.shard_map(
        body,
        mesh=mesh,
        in_specs=in_specs,
        out_specs=P(("groups", "ctx"), None),
        check_vma=False,
    )
```

time: 305 us -> 168 us (0.55)
  waiting for transfers between devices: 156 us -> 108 us
  loops' own time: 45 us -> 0 us
  local copies, waits for them, and re-layouts: 44.8 us -> 16.1 us
  Pallas kernels: 0 us -> 17.1 us
  other arithmetic: 21.9 us -> 5.02 us
  matrix products: 21.3 us -> 4.63 us
    all_gather x2 -> x1, waiting for transfers between devices: 78.7 us -> 30.9 us  [body(): kv = lax.all_gather(local, 'ctx', axis=0, tiled=True)[None]]
    another operation x3 -> x0, loops' own time: 45 us -> none  [the longest x2 43.1 us: attend_unit(): lax.fori_loop(0, group_count, fill_turn, (start_scores, start_values))]
    dynamic_slice x37 -> x1, local copies, waits for them, and re-layouts: 31.7 us -> 1.24 us  [body(): low = span_pairs[me]]
    pallas_call x0 -> x1, Pallas kernels: none -> 17.1 us  [attend(): pl.pallas_call(functools.partial(attend_kernel, n), out_shape=jax.ShapeDt...]
    dot_general x10 -> x0, matrix products: 16.7 us -> none  [the longest x8 14.2 us: fill_turn(): jnp.einsum('qhgd,khd->qhgk', query_heads, key_part, preferred_element_typ...]
    reduce_sum x3 -> x0, other arithmetic: 9.33 us -> none  [the longest x2 9.22 us: attend_unit(): totals = jnp.sum(weights.astype(jnp.float32), axis=(0, 4))]
    concatenate x10 -> x4, local copies, waits for them, and re-layouts: 0.85 us -> 9.7 us  [turn(): swapped = jnp.concatenate([x[..., HD // 2:], x[..., :HD // 2]], axis=-1)]
    dynamic_update_slice x10 -> x0, local copies, waits for them, and re-layouts: 8.12 us -> none  [the longest x8 6.45 us: fill_turn(): lax.dynamic_update_index_in_dim(value_store, value_part, turn_index, 0)]
  transfers between devices with their start and end apart: 3 -> 2, of which waited for: 3 -> 2; matrix products, arithmetic and copies ran while one was open for 2% -> 11% of each run, Pallas kernels for 0% -> 0%
where the time goes in v1:
time: 168 us; the launch traced here: 166 us
  waiting for transfers between devices  108 us (64%)
  Pallas kernels  17.1 us (10%)
  local copies, waits for them, and re-layouts  16.1 us (10%)
  between operations  14.9 us (9%)
  other arithmetic  5.02 us (3%)
  matrix products  4.63 us (3%)
    all_gather x1, waiting for transfers between devices, body(): lax.all_gather(cache_weight, 'ctx', axis=0, tiled=True)  76.5 us
    all_gather x1, waiting for transfers between devices, body(): kv = lax.all_gather(local, 'ctx', axis=0, tiled=True)[None]  30.9 us
    pallas_call x1, Pallas kernels, attend(): pl.pallas_call(functools.partial(attend_kernel, n), out_shape=jax.ShapeDt...  17.1 us
    concatenate x4, local copies, waits for them, and re-layouts, turn(): swapped = jnp.concatenate([x[..., HD // 2:], x[..., :HD // 2]], axis=-1)  9.7 us
    dot_general x1, matrix products, body(): jnp.dot(hidden, lax.all_gather(cache_weight, 'ctx', axis=0, tiled=True),...  4.63 us
  transfers between devices with their start and end apart: 2, of which 2 were waited for; matrix products, arithmetic and copies ran while one was open for 11% of the time, Pallas kernels for 0%

profile of v1, /device:TPU:1, one launch (start us, length us, event | category | flops | bytes accessed | tf_op | source)
XLA Modules:
  0.0 166.0 jit_solution(13218405396090154840)
XLA Ops:
  6.5 0.7 all-gather.3.cloned.1.call-update
  7.3 0.0 all-gather.5.cloned.1.call-start
  7.3 1.2 dynamic_slice.3
  9.9 0.1 add_convert_fusion
  10.0 0.3 multiply_cosine_fusion
  10.3 0.1 pad_maximum_fusion.3
  10.4 0.1 pad_maximum_fusion.4
  10.5 76.5 %all-gather.3.cloned.1.call-done = bf16[4096,1024]{1,0:T(8,128)(2,1)} async-done(((bf16[256,1024]{1,0:T(8,128)(2,1)}), bf16[4096,1024]{1,0:T(8,128)(2,1)}) %all-gather.3.cloned.1.call-update) | async-done | bytes 8388624 | tf_op jit(solution)/shard_map/all_gather | solution.py:159
  87.0 4.6 %fusion.8 = f32[128,1024]{1,0:T(8,128)S(1)} fusion(bf16[128,4096]{1,0:T(8,128)(2,1)S(1)} %copy-done, bf16[4096,1024]{1,0:T(8,128)(2,1)} %all-gather.3.cloned.1.call-done), kind=kOutput, calls=%fused_computation.28 | convolution fusion | flops 1073741824 | bytes 9961472 | tf_op jit(solution)/shard_map/dot_general | solution.py:157
  91.7 0.1 reshape.88
  91.8 0.2 fusion.7
  92.0 0.2 maximum_multiply_fusion.1
  92.2 0.1 fusion.3
  92.3 0.7 pad_maximum_fusion
  93.1 0.1 convert_element_type.21
  93.1 0.1 copy.12.pattern_ref
  93.2 1.5 copy.13
  94.7 1.5 fusion.6
  96.2 2.5 %concatenate.37 = f32[2,64,32,64]{1,0,3,2:T(2,128)S(1)} reshape(f32[128,32,64]{0,2,1:T(8,128)} %get-tuple-element.6) | data formatting | bytes 2097152 | tf_op jit(solution)/shard_map/concatenate | solution.py:154
  98.7 2.4 %copy.11 = f32[2,64,32,64]{3,1,2,0:T(8,128)} copy(f32[2,64,32,64]{1,0,3,2:T(2,128)S(1)} %concatenate.37) | data formatting | bytes 2097152 | tf_op jit(solution)/shard_map/concatenate | solution.py:154
  101.0 2.5 %concatenate.36 = f32[2,64,32,64]{1,0,3,2:T(2,128)S(1)} reshape(f32[128,32,64]{0,2,1:T(8,128)} %get-tuple-element.5) | data formatting | bytes 2097152 | tf_op jit(solution)/shard_map/concatenate | solution.py:154
  103.5 2.3 %copy.10 = f32[2,64,32,64]{3,1,2,0:T(8,128)} copy(f32[2,64,32,64]{1,0,3,2:T(2,128)S(1)} %concatenate.36) | data formatting | bytes 2097152 | tf_op jit(solution)/shard_map/concatenate | solution.py:154
  105.9 1.4 convert_bitcast_fusion
  107.3 0.4 copy.14
  107.7 0.3 multiply_cosine_fusion.1
  108.0 0.1 pad_maximum_fusion.1
  108.1 0.1 pad_maximum_fusion.2
  108.2 0.7 copy-done.2
  108.9 0.6 copy-done.3
  109.6 1.5 fusion.2.rot_ref
  111.1 30.9 %all-gather.5.cloned.1.call-done = bf16[2048,1024]{1,0:T(8,128)(2,1)} async-done(((bf16[128,1024]{1,0:T(8,128)(2,1)}), bf16[2048,1024]{1,0:T(8,128)(2,1)}) %all-gather.5.cloned.1.call-update) | async-done | bytes 4194320 | tf_op jit(solution)/shard_map/all_gather | solution.py:164
  142.0 17.1 %shard_map.55 = bf16[128,4096]{1,0:T(8,128)(2,1)} custom-call(s32[16,7]{1,0:T(8,128)S(1)} %copy.12.pattern_ref, s32[16]{0:T(128)S(1)} %copy-done.1, bf16[2,32,64,128]{3,2,1,0:T(8,128)(2,1)S(1)} %fusion.2.rot_ref, bf16[1,2048,1024]{2,1,0:T(8,128)(2,1)} %bitcast.28), custom_call_target="tpu_custom_call" | custom-call | tf_op jit(solution)/shard_map/pallas_call | solution.py:127
  (15 shorter events, 0.1 us)
Async XLA Ops:
  6.5 80.4 %copy-start = (bf16[128,4096]{1,0:T(8,128)(2,1)S(1)}, bf16[128,4096]{1,0:T(8,128)(2,1)}, u32[]{:S(2)}) copy-start(bf16[128,4096]{1,0:T(8,128)(2,1)} %param.5) | copy-start | bytes 3145732
  6.5 80.4 %all-gather.3.cloned.1.call-start = ((), (), s32[]{:S(2)}) async-start(), calls=%async_computation | async-start | bytes 8912896 | tf_op jit(solution)/shard_map/all_gather | solution.py:159
  7.3 134.8 %all-gather.5.cloned.1.call-start = ((), (), s32[]{:S(2)}) async-start(), calls=%async_computation.1 | async-start | bytes 4456448 | tf_op jit(solution)/shard_map/all_gather | solution.py:164
  91.8 1.4 copy-start.4
  107.3 1.6 copy-start.2
  107.3 2.2 %copy-start.3 = (f32[2,64,32,64]{3,1,2,0:T(8,128)S(1)}, f32[2,64,32,64]{3,1,2,0:T(8,128)}, u32[]{:S(2)}) copy-start(f32[2,64,32,64]{3,1,2,0:T(8,128)} %copy.10) | copy-start | bytes 3145732
  109.6 32.5 %copy-start.1 = (s32[16]{0:T(128)S(1)}, s32[16]{0:T(128)}, u32[]{:S(2)}) copy-start(s32[16]{0:T(128)} %spans_ref.1) | copy-start | bytes 196
Sparse Core Ops, SparseCore 0:
  9.5 77.3 all-gather.2
  93.2 48.7 all-gather.4

commit v2 on v1

--- a/solution.py
+++ b/solution.py
@@ -139,7 +139,278 @@
     )(pattern, span_pairs, rotated, kv)
 
 
-def body(hidden, queries, cache_weight, pattern, span_pairs):
+MESH = pl.DeviceIdType.MESH
+KBLOCK = 512
+
+
+def project_kernel(
+    n,
+    groups,
+    weight_ref,
+    hidden_ref,
+    queries_ref,
+    table_ref,
+    rot_ref,
+    kv_ref,
+    weights,
+    states,
+    asked,
+    tables,
+    product,
+    outgoing,
+    sems,
+    kv_sems,
+    side_sems,
+    kv_side_sems,
+    own_sems,
+    kv_own_sems,
+    peer_sems,
+    table_sems,
+    kv_peer_sems,
+    local_sems,
+):
+    g = lax.axis_index("groups")
+    me = lax.axis_index("ctx")
+    chips = n // 2
+    half = chips // 2
+    chip, core = me // 2, me % 2
+    depth, width = weight_ref.shape[0], weights.shape[1]
+    tok_rows = hidden_ref.shape[0]
+    span = tok_rows // 2
+    cut = depth // 2
+
+    if chips > 8:
+        spot = chip
+    else:
+        spot = (1 - chip % 2) * (chip // 2) + (chip % 2) * (chips - 1 - chip // 2)
+
+    def index(position, which):
+        p = (position + chips) % chips
+        if chips > 8:
+            return p * 2 + which
+        back = p // half
+        return 2 * ((1 - back) * 2 * p + back * (2 * (chips - 1 - p) + 1)) + which
+
+    sibling = (g, chip * 2 + 1 - core)
+    ring = ((g, index(spot + 1, core)), (g, index(spot - 1, core)))
+    peers = [((g + d) % groups, me) for d in range(1, groups)]
+
+    barrier = pltpu.get_barrier_semaphore()
+    for device in (sibling, *ring, *peers):
+        pl.semaphore_signal(barrier, inc=1, device_id=device, device_id_type=MESH)
+    pl.semaphore_wait(barrier, 3 + len(peers))
+
+    started = []
+
+    def copy(source, target, send, receive, device):
+        return pltpu.make_async_remote_copy(
+            src_ref=source,
+            dst_ref=target,
+            send_sem=send,
+            recv_sem=receive,
+            device_id=device,
+            device_id_type=MESH,
+        )
+
+    def send(*args):
+        c = copy(*args)
+        c.start()
+        started.append(c)
+
+    def gather(place, first, pieces, ready, ring_sems, across, own, between):
+        def used(d, k, i):
+            if k < half - 1:
+                return True
+            return (i < pieces // 2) == (d == 0)
+
+        for i in range(pieces):
+            ready(i)
+            for d in range(2):
+                if used(d, 0, i):
+                    send(
+                        first(i), place(me, i), ring_sems.at[0, d, 0, i],
+                        ring_sems.at[1, d, 0, i], ring[d],
+                    )
+            send(first(i), place(me, i), own.at[0, i], own.at[1, i], sibling)
+        between()
+        for k in range(1, half + 1):
+            for i in range(pieces):
+                for d in range(2):
+                    if not used(d, k - 1, i):
+                        continue
+                    at = place(index(spot - k if d == 0 else spot + k, core), i)
+                    s, r = ring_sems.at[0, d, k - 1, i], ring_sems.at[1, d, k - 1, i]
+                    copy(at, at, s, r, ring[d]).wait_recv()
+                    if k < half and used(d, k, i):
+                        send(at, at, ring_sems.at[0, d, k, i], ring_sems.at[1, d, k, i], ring[d])
+                    send(at, at, across.at[0, d, k - 1, i], across.at[1, d, k - 1, i], sibling)
+        for i in range(pieces):
+            at = place(sibling[1], i)
+            copy(at, at, own.at[0, i], own.at[1, i], sibling).wait_recv()
+        for k in range(1, half + 1):
+            for i in range(pieces):
+                for d in range(2):
+                    if used(d, k - 1, i):
+                        at = place(index(spot - k if d == 0 else spot + k, 1 - core), i)
+                        s, r = across.at[0, d, k - 1, i], across.at[1, d, k - 1, i]
+                        copy(at, at, s, r, sibling).wait_recv()
+
+    columns = pl.ds(pl.multiple_of(g * width, width), width)
+
+    def weight_place(slot, i):
+        return weights.at[pl.ds(pl.multiple_of(slot * depth + i * cut, cut), cut), :]
+
+    locals_ = [
+        pltpu.make_async_copy(
+            weight_ref.at[:, columns],
+            weights.at[pl.ds(pl.multiple_of(me * depth, depth), depth), :],
+            local_sems.at[0],
+        ),
+        pltpu.make_async_copy(hidden_ref, states.at[g], local_sems.at[1]),
+        pltpu.make_async_copy(queries_ref, asked, local_sems.at[2]),
+        pltpu.make_async_copy(table_ref, tables.at[g], local_sems.at[3]),
+    ]
+
+    def between():
+        for d, device in enumerate(peers):
+            send(hidden_ref, states.at[g], peer_sems.at[0, d], peer_sems.at[1, d], device)
+            send(table_ref, tables.at[g], table_sems.at[0, d], table_sems.at[1, d], device)
+        for c in locals_:
+            c.start()
+        for c in locals_:
+            c.wait()
+
+        def rotate(h, carry):
+            x = asked[:, pl.ds(pl.multiple_of(h * HD, HD), HD)].astype(jnp.float32)
+            y = x * tables[g, 0] + pltpu.roll(x, HD // 2, 1) * tables[g, 1]
+            y = y.astype(jnp.bfloat16)
+            rot_ref[0, h] = y[:span]
+            rot_ref[1, h] = y[span:]
+            return carry
+
+        lax.fori_loop(0, QH, rotate, 0)
+
+    gather(
+        weight_place,
+        lambda i: weight_ref.at[pl.ds(i * cut, cut), columns],
+        2,
+        lambda i: None,
+        sems,
+        side_sems,
+        own_sems,
+        between,
+    )
+    for d in range(groups - 1):
+        source = (g + groups - 1 - d) % groups
+        copy(
+            states.at[source], states.at[source], peer_sems.at[0, d], peer_sems.at[1, d], peers[d]
+        ).wait_recv()
+        copy(
+            tables.at[source], tables.at[source], table_sems.at[0, d], table_sems.at[1, d], peers[d]
+        ).wait_recv()
+
+    product[...] = jnp.zeros_like(product)
+
+    def multiply(k, carry):
+        at = pl.ds(pl.multiple_of(k * KBLOCK, KBLOCK), KBLOCK)
+        x = states[:, :, at].reshape(groups * tok_rows, KBLOCK)
+        product[...] += jnp.dot(
+            x, weights[at, :], preferred_element_type=jnp.float32
+        ).reshape(product.shape)
+        return carry
+
+    lax.fori_loop(0, states.shape[2] // KBLOCK, multiply, 0)
+
+    is_key = g * width < KVH * HD
+
+    def finish(which, store):
+        for h in range(width // HD):
+            x = product[which, :, h * HD : (h + 1) * HD]
+            y = x * tables[which, 0] + pltpu.roll(x, HD // 2, 1) * tables[which, 1]
+            store(h, jnp.where(is_key, y, x).astype(jnp.bfloat16))
+
+    def store_own(h, value):
+        kv_ref[g, me, :, h * HD : (h + 1) * HD] = value
+
+    finish(g, store_own)
+
+    def share():
+        for d, device in enumerate(peers):
+
+            def store(h, value, d=d):
+                outgoing[d, :, h * HD : (h + 1) * HD] = value
+
+            finish(device[0], store)
+            send(
+                outgoing.at[d], kv_ref.at[g, me], kv_peer_sems.at[0, d], kv_peer_sems.at[1, d],
+                device,
+            )
+
+    def kv_place(slot, i):
+        return kv_ref.at[(g + i) % groups, slot]
+
+    def ready(i):
+        if i == 1:
+            share()
+        if i:
+            at = kv_place(me, i)
+            d = groups - i - 1
+            copy(at, at, kv_peer_sems.at[0, d], kv_peer_sems.at[1, d], peers[d]).wait_recv()
+
+    gather(
+        kv_place,
+        lambda i: kv_place(me, i),
+        groups,
+        ready,
+        kv_sems,
+        kv_side_sems,
+        kv_own_sems,
+        lambda: None,
+    )
+    for c in started:
+        c.wait_send()
+
+
+def project(n, groups, weight, hidden, queries, table):
+    depth, width = weight.shape[0], weight.shape[1] // groups
+    tok_rows, wide = hidden.shape
+    half = n // 4
+    whole = pl.BlockSpec(memory_space=pl.ANY)
+    vmem = pl.BlockSpec(memory_space=pltpu.VMEM)
+    dma = pltpu.SemaphoreType.DMA
+    return pl.pallas_call(
+        functools.partial(project_kernel, n, groups),
+        out_shape=(
+            jax.ShapeDtypeStruct((2, QH, tok_rows // 2, HD), jnp.bfloat16),
+            jax.ShapeDtypeStruct((groups, n, tok_rows, width), jnp.bfloat16),
+        ),
+        in_specs=[whole, whole, whole, whole],
+        out_specs=(vmem, vmem),
+        scratch_shapes=[
+            pltpu.VMEM((n * depth, width), jnp.bfloat16),
+            pltpu.VMEM((groups, tok_rows, wide), jnp.bfloat16),
+            pltpu.VMEM(queries.shape, jnp.bfloat16),
+            pltpu.VMEM((groups, *table.shape), jnp.float32),
+            pltpu.VMEM((groups, tok_rows, width), jnp.float32),
+            pltpu.VMEM((groups - 1, tok_rows, width), jnp.bfloat16),
+            dma((2, 2, half, 2)),
+            dma((2, 2, half, groups)),
+            dma((2, 2, half, 2)),
+            dma((2, 2, half, groups)),
+            dma((2, 2)),
+            dma((2, groups)),
+            dma((2, groups - 1)),
+            dma((2, groups - 1)),
+            dma((2, groups - 1)),
+            dma((4,)),
+        ],
+        compiler_params=pltpu.CompilerParams(
+            collective_id=0, has_side_effects=True, vmem_limit_bytes=48 * 1024 * 1024
+        ),
+    )(weight, hidden, queries, table)
+
+
+def body(groups, hidden, queries, cache_weight, pattern, span_pairs):
     tok_rows = hidden.shape[0]
     n = lax.axis_size("ctx")
     me = lax.axis_index("ctx")
@@ -147,23 +418,9 @@
     low = span_pairs[me]
     offsets = jnp.arange(span, dtype=jnp.int32)
     positions = jnp.concatenate([low * span + offsets, (2 * n - 1 - low) * span + offsets])
-    cosine, sine = rope_tables(positions)
-
-    def turn(x, heads):
-        x = x.reshape(tok_rows, heads, HD)
-        swapped = jnp.concatenate([x[..., HD // 2 :], x[..., : HD // 2]], axis=-1)
-        return x * cosine[:, None] + swapped * sine[:, None]
-
-    projected = jnp.dot(
-        hidden,
-        lax.all_gather(cache_weight, "ctx", axis=0, tiled=True),
-        preferred_element_type=jnp.float32,
-    )
-    keys = turn(projected[:, : KVH * HD], KVH).reshape(tok_rows, KVH * HD)
-    local = jnp.concatenate([keys, projected[:, KVH * HD :]], axis=1).astype(jnp.bfloat16)
-    kv = lax.all_gather(local, "ctx", axis=0, tiled=True)[None]
-    rotated = turn(queries.astype(jnp.float32), QH).astype(jnp.bfloat16)
-    rotated = rotated.reshape(2, span, QH, HD).transpose(0, 2, 1, 3)
+    table = jnp.stack(rope_tables(positions))
+    rotated, kv = project(n, groups, cache_weight, hidden, queries, table)
+    kv = kv.reshape(groups, n * tok_rows, kv.shape[3])
     return attend(n, pattern, span_pairs, rotated, kv, tok_rows)
 
 
@@ -176,7 +433,7 @@
         P("groups"),
     )
     return jax.shard_map(
-        body,
+        functools.partial(body, mesh.shape["groups"]),
         mesh=mesh,
         in_specs=in_specs,
         out_specs=P(("groups", "ctx"), None),

time: 168 us -> 90.6 us (0.54)
  the two profiles are of different devices: /device:TPU:1 before, /device:TPU:0 now
where the time goes in v2:
time: 90.6 us; the launch traced here: 90.2 us
  Pallas kernels  82.1 us (91%)
  local copies, waits for them, and re-layouts  6.14 us (7%)
  between operations  1.36 us (2%)
    pallas_call x1, Pallas kernels, project(): pl.pallas_call(functools.partial(project_kernel, n, groups), out_shape=(j...  62.9 us
    pallas_call x1, Pallas kernels, attend(): pl.pallas_call(functools.partial(attend_kernel, n), out_shape=jax.ShapeDt...  19.3 us
    unnamed x9, local copies, waits for them, and re-layouts  4.9 us

profile of v2, /device:TPU:0, one launch (start us, length us, event | category | flops | bytes accessed | tf_op | source)
XLA Modules:
  0.0 90.2 jit_solution(1446690734435173984)
XLA Ops:
  0.0 1.2 %dynamic_slice.3 = s32[1]{0:T(128)} dynamic-slice(s32[16]{0:T(128)} %spans_ref.1, s32[]{:T(128)S(6)} %select_n.3), dynamic_slice_sizes={1} | dynamic-slice | bytes 12 | tf_op jit(solution)/shard_map/dynamic_slice | solution.py:418
  2.5 0.1 add_convert_fusion
  2.6 0.8 copy.6.pattern_ref
  3.4 0.3 multiply_cosine_fusion
  3.7 0.1 maximum_bitcast_fusion
  3.8 0.1 maximum_bitcast_fusion.1
  3.9 0.0 copy-start
  3.9 1.2 %copy-done = bf16[128,4096]{1,0:T(8,128)(2,1)S(1)} copy-done((bf16[128,4096]{1,0:T(8,128)(2,1)S(1)}, bf16[128,4096]{1,0:T(8,128)(2,1)}, u32[]{:S(2)}) %copy-start) | copy-done | bytes 1048600
  5.1 0.0 copy-start.1
  5.1 1.2 %copy-done.1 = bf16[128,4096]{1,0:T(8,128)(2,1)S(1)} copy-done((bf16[128,4096]{1,0:T(8,128)(2,1)S(1)}, bf16[128,4096]{1,0:T(8,128)(2,1)}, u32[]{:S(2)}) %copy-start.1) | copy-done | bytes 1048600
  6.4 0.0 copy-start.2
  6.4 1.0 %copy-done.2 = bf16[256,1024]{1,0:T(8,128)(2,1)S(1)} copy-done((bf16[256,1024]{1,0:T(8,128)(2,1)S(1)}, bf16[256,1024]{1,0:T(8,128)(2,1)}, u32[]{:S(2)}) %copy-start.2) | copy-done | bytes 524312
  7.4 62.9 %shard_map.55 = (bf16[2,32,64,128]{3,2,1,0:T(8,128)(2,1)S(1)}, bf16[2,16,128,512]{3,2,1,0:T(8,128)(2,1)}) custom-call(bf16[256,1024]{1,0:T(8,128)(2,1)S(1)} %copy-done.2, bf16[128,4096]{1,0:T(8,128)(2,1)S(1)} %copy-done, bf16[128,4096]{1,0:T(8,128)(2,1)S(1)} %copy-done.1, f32[2,128,128]{2,1,0:T(8,128)S(1)} %pad_maximum_fusion.table_ref), custom_call_target="tpu_custom_call" | custom-call | tf_op jit(solution)/shard_map/pallas_call | solution.py:381
  70.3 0.0 copy-start.3
  70.3 0.6 copy-done.3
  70.9 19.3 %shard_map.56 = bf16[128,4096]{1,0:T(8,128)(2,1)} custom-call(s32[16,7]{1,0:T(8,128)S(1)} %copy.6.pattern_ref, s32[16]{0:T(128)S(1)} %copy-done.3, bf16[2,32,64,128]{3,2,1,0:T(8,128)(2,1)S(1)} %get-tuple-element.7.rot_ref, bf16[2,2048,512]{2,1,0:T(8,128)(2,1)} %bitcast.7), custom_call_target="tpu_custom_call" | custom-call | tf_op jit(solution)/shard_map/pallas_call | solution.py:127
  (3 shorter events, 0.0 us)
Async XLA Ops:
  3.9 1.2 %copy-start = (bf16[128,4096]{1,0:T(8,128)(2,1)S(1)}, bf16[128,4096]{1,0:T(8,128)(2,1)}, u32[]{:S(2)}) copy-start(bf16[128,4096]{1,0:T(8,128)(2,1)} %hidden_ref.1) | copy-start | bytes 3145732
  5.1 1.2 %copy-start.1 = (bf16[128,4096]{1,0:T(8,128)(2,1)S(1)}, bf16[128,4096]{1,0:T(8,128)(2,1)}, u32[]{:S(2)}) copy-start(bf16[128,4096]{1,0:T(8,128)(2,1)} %queries_ref.1) | copy-start | bytes 3145732
  6.4 1.0 %copy-start.2 = (bf16[256,1024]{1,0:T(8,128)(2,1)S(1)}, bf16[256,1024]{1,0:T(8,128)(2,1)}, u32[]{:S(2)}) copy-start(bf16[256,1024]{1,0:T(8,128)(2,1)} %weight_ref.1) | copy-start | bytes 1572868
  70.3 0.7 copy-start.3

commit v3 on v2

--- a/solution.py
+++ b/solution.py
@@ -15,17 +15,6 @@
 ROPE_BASE = 500000.0
 MASKED = -1e30
 CHUNK = 2 * BLOCK
-
-
-def rope_tables(positions):
-    half = HD // 2
-    frequency = ROPE_BASE ** (-(jnp.arange(half, dtype=jnp.float32) * 2.0 / HD))
-    angles = positions.astype(jnp.float32)[:, None] * frequency[None, :]
-    cosine, sine = jnp.cos(angles), jnp.sin(angles)
-    return (
-        jnp.concatenate([cosine, cosine], axis=1),
-        jnp.concatenate([-sine, sine], axis=1),
-    )
 
 
 def attend_kernel(
@@ -135,7 +124,7 @@
             pltpu.VMEM((chunks, rows, CHUNK), jnp.float32),
             pltpu.SMEM((n,), jnp.int32),
         ],
-        compiler_params=pltpu.CompilerParams(vmem_limit_bytes=52 * 1024 * 1024),
+        compiler_params=pltpu.CompilerParams(vmem_limit_bytes=24 * 1024 * 1024),
     )(pattern, span_pairs, rotated, kv)
 
 
@@ -149,7 +138,8 @@
     weight_ref,
     hidden_ref,
     queries_ref,
-    table_ref,
+    spans_ref,
+    frequency_ref,
     rot_ref,
     kv_ref,
     weights,
@@ -268,15 +258,25 @@
         ),
         pltpu.make_async_copy(hidden_ref, states.at[g], local_sems.at[1]),
         pltpu.make_async_copy(queries_ref, asked, local_sems.at[2]),
-        pltpu.make_async_copy(table_ref, tables.at[g], local_sems.at[3]),
     ]
 
     def between():
         for d, device in enumerate(peers):
             send(hidden_ref, states.at[g], peer_sems.at[0, d], peer_sems.at[1, d], device)
-            send(table_ref, tables.at[g], table_sems.at[0, d], table_sems.at[1, d], device)
         for c in locals_:
             c.start()
+        low = spans_ref[me]
+        line = lax.broadcasted_iota(jnp.int32, (tok_rows, HD), 0)
+        place = jnp.where(line < span, low * span, (2 * n - 2 - low) * span) + line
+        angles = place.astype(jnp.float32) * frequency_ref[...]
+        lane = lax.broadcasted_iota(jnp.int32, (tok_rows, HD), 1)
+        sine = jnp.sin(angles)
+        tables[g, 0] = jnp.cos(angles)
+        tables[g, 1] = jnp.where(lane < HD // 2, -sine, sine)
+        for d, device in enumerate(peers):
+            send(
+                tables.at[g], tables.at[g], table_sems.at[0, d], table_sems.at[1, d], device
+            )
         for c in locals_:
             c.wait()
 
@@ -371,11 +371,15 @@
         c.wait_send()
 
 
-def project(n, groups, weight, hidden, queries, table):
+def project(n, groups, weight, hidden, queries, span_pairs):
     depth, width = weight.shape[0], weight.shape[1] // groups
     tok_rows, wide = hidden.shape
     half = n // 4
-    whole = pl.BlockSpec(memory_space=pl.ANY)
+    half_ids = jnp.arange(HD // 2, dtype=jnp.float32)
+    frequency = ROPE_BASE ** (-(half_ids * 2.0 / HD))
+    frequency = jnp.concatenate([frequency, frequency])[None]
+    hbm = pl.BlockSpec(memory_space=pltpu.HBM)
+    smem = pl.BlockSpec(memory_space=pltpu.SMEM)
     vmem = pl.BlockSpec(memory_space=pltpu.VMEM)
     dma = pltpu.SemaphoreType.DMA
     return pl.pallas_call(
@@ -384,13 +388,13 @@
             jax.ShapeDtypeStruct((2, QH, tok_rows // 2, HD), jnp.bfloat16),
             jax.ShapeDtypeStruct((groups, n, tok_rows, width), jnp.bfloat16),
         ),
-        in_specs=[whole, whole, whole, whole],
+        in_specs=[hbm, hbm, hbm, smem, vmem],
         out_specs=(vmem, vmem),
         scratch_shapes=[
             pltpu.VMEM((n * depth, width), jnp.bfloat16),
             pltpu.VMEM((groups, tok_rows, wide), jnp.bfloat16),
             pltpu.VMEM(queries.shape, jnp.bfloat16),
-            pltpu.VMEM((groups, *table.shape), jnp.float32),
+            pltpu.VMEM((groups, 2, tok_rows, HD), jnp.float32),
             pltpu.VMEM((groups, tok_rows, width), jnp.float32),
             pltpu.VMEM((groups - 1, tok_rows, width), jnp.bfloat16),
             dma((2, 2, half, 2)),
@@ -402,24 +406,18 @@
             dma((2, groups - 1)),
             dma((2, groups - 1)),
             dma((2, groups - 1)),
-            dma((4,)),
+            dma((3,)),
         ],
         compiler_params=pltpu.CompilerParams(
-            collective_id=0, has_side_effects=True, vmem_limit_bytes=48 * 1024 * 1024
+            collective_id=0, has_side_effects=True, vmem_limit_bytes=24 * 1024 * 1024
         ),
-    )(weight, hidden, queries, table)
+    )(weight, hidden, queries, span_pairs, frequency)
 
 
 def body(groups, hidden, queries, cache_weight, pattern, span_pairs):
     tok_rows = hidden.shape[0]
     n = lax.axis_size("ctx")
-    me = lax.axis_index("ctx")
-    span = tok_rows // 2
-    low = span_pairs[me]
-    offsets = jnp.arange(span, dtype=jnp.int32)
-    positions = jnp.concatenate([low * span + offsets, (2 * n - 1 - low) * span + offsets])
-    table = jnp.stack(rope_tables(positions))
-    rotated, kv = project(n, groups, cache_weight, hidden, queries, table)
+    rotated, kv = project(n, groups, cache_weight, hidden, queries, span_pairs)
     kv = kv.reshape(groups, n * tok_rows, kv.shape[3])
     return attend(n, pattern, span_pairs, rotated, kv, tok_rows)
 

time: 90.6 us -> 83.9 us (0.926)
  the two profiles are of different devices: /device:TPU:0 before, /device:TPU:1 now
where the time goes in v3:
time: 83.9 us; the launch traced here: 84.3 us
  Pallas kernels  79.3 us (95%)
  local copies, waits for them, and re-layouts  4.91 us (6%)
    pallas_call x1, Pallas kernels, project(): pl.pallas_call(functools.partial(project_kernel, n, groups), out_shape=(j...  61.5 us
    pallas_call x1, Pallas kernels, attend(): pl.pallas_call(functools.partial(attend_kernel, n), out_shape=jax.ShapeDt...  17.8 us
    unnamed x9, local copies, waits for them, and re-layouts  4.91 us

profile of v3, /device:TPU:1, one launch (start us, length us, event | category | flops | bytes accessed | tf_op | source)
XLA Modules:
  0.0 84.3 jit_solution(670504558012454907)
XLA Ops:
  0.0 0.1 maximum_bitcast_fusion.frequency_ref
  0.1 0.8 copy.6.pattern_ref
  0.9 0.0 copy-start
  0.9 1.2 %copy-done = bf16[128,4096]{1,0:T(8,128)(2,1)S(1)} copy-done((bf16[128,4096]{1,0:T(8,128)(2,1)S(1)}, bf16[128,4096]{1,0:T(8,128)(2,1)}, u32[]{:S(2)}) %copy-start) | copy-done | bytes 1048600
  2.1 0.0 copy-start.1
  2.1 1.2 %copy-done.1 = bf16[128,4096]{1,0:T(8,128)(2,1)S(1)} copy-done((bf16[128,4096]{1,0:T(8,128)(2,1)S(1)}, bf16[128,4096]{1,0:T(8,128)(2,1)}, u32[]{:S(2)}) %copy-start.1) | copy-done | bytes 1048600
  3.3 0.0 copy-start.2
  3.3 1.0 %copy-done.2 = bf16[256,1024]{1,0:T(8,128)(2,1)S(1)} copy-done((bf16[256,1024]{1,0:T(8,128)(2,1)S(1)}, bf16[256,1024]{1,0:T(8,128)(2,1)}, u32[]{:S(2)}) %copy-start.2) | copy-done | bytes 524312
  4.3 0.0 copy-start.3
  4.4 0.7 copy-done.3
  5.0 61.5 %shard_map.55 = (bf16[2,32,64,128]{3,2,1,0:T(8,128)(2,1)S(1)}, bf16[2,16,128,512]{3,2,1,0:T(8,128)(2,1)S(1)}) custom-call(bf16[256,1024]{1,0:T(8,128)(2,1)S(1)} %copy-done.2, bf16[128,4096]{1,0:T(8,128)(2,1)S(1)} %copy-done, bf16[128,4096]{1,0:T(8,128)(2,1)S(1)} %copy-done.1, s32[16]{0:T(128)S(1)} %copy-done.3, f32[1,128]{1,0:T(1,128)S(1)} %maximum_bitcast_fusion.frequency_ref), custom_call_target="tpu_custom_call" | custom-call | tf_op jit(solution)/shard_map/pallas_call | solution.py:385
  66.5 17.8 %shard_map.56 = bf16[128,4096]{1,0:T(8,128)(2,1)} custom-call(s32[16,7]{1,0:T(8,128)S(1)} %copy.6.pattern_ref, s32[16]{0:T(128)S(1)} %copy-done.3, bf16[2,32,64,128]{3,2,1,0:T(8,128)(2,1)S(1)} %get-tuple-element.7.rot_ref, bf16[2,2048,512]{2,1,0:T(8,128)(2,1)S(1)} %bitcast.3), custom_call_target="tpu_custom_call" | custom-call | tf_op jit(solution)/shard_map/pallas_call | solution.py:116
  (1 shorter events, 0.0 us)
Async XLA Ops:
  0.9 1.2 %copy-start = (bf16[128,4096]{1,0:T(8,128)(2,1)S(1)}, bf16[128,4096]{1,0:T(8,128)(2,1)}, u32[]{:S(2)}) copy-start(bf16[128,4096]{1,0:T(8,128)(2,1)} %hidden_ref.1) | copy-start | bytes 3145732
  2.1 1.2 %copy-start.1 = (bf16[128,4096]{1,0:T(8,128)(2,1)S(1)}, bf16[128,4096]{1,0:T(8,128)(2,1)}, u32[]{:S(2)}) copy-start(bf16[128,4096]{1,0:T(8,128)(2,1)} %queries_ref.1) | copy-start | bytes 3145732
  3.3 1.0 %copy-start.2 = (bf16[256,1024]{1,0:T(8,128)(2,1)S(1)}, bf16[256,1024]{1,0:T(8,128)(2,1)}, u32[]{:S(2)}) copy-start(bf16[256,1024]{1,0:T(8,128)(2,1)} %weight_ref.1) | copy-start | bytes 1572868
  4.3 0.7 copy-start.3

commit v4 on v3

--- a/solution.py
+++ b/solution.py
@@ -15,6 +15,44 @@
 ROPE_BASE = 500000.0
 MASKED = -1e30
 CHUNK = 2 * BLOCK
+
+
+def attend_long(part, count, chunks, offset, span, group, rot_ref, kbuf, vbuf, scores, out_ref):
+    rows = group * span
+    factor = HD ** (-0.5) * math.log2(math.e)
+    for h in range(KVH):
+        query = rot_ref[part, h * group : (h + 1) * group].reshape(rows, HD)
+
+        def score(c, peak):
+            keys = kbuf[h, pl.ds(pl.multiple_of(c * CHUNK, CHUNK), CHUNK), :]
+            s = lax.dot_general(
+                query, keys, (((1,), (1,)), ((), ())), preferred_element_type=jnp.float32
+            )
+            col = c * CHUNK + lax.broadcasted_iota(jnp.int32, (span, CHUNK), 1)
+            line = offset + lax.broadcasted_iota(jnp.int32, (span, CHUNK), 0)
+            live = (col < count * BLOCK) & ((col >= BLOCK) | (col <= line))
+            bias = jnp.where(live, 0.0, MASKED)
+            s = (s.reshape(group, span, CHUNK) + bias[None]).reshape(rows, CHUNK)
+            scores[c] = s
+            return jnp.maximum(peak, jnp.maximum(s[:, :BLOCK], s[:, BLOCK:]))
+
+        peak = lax.fori_loop(
+            0, chunks, score, jnp.full((rows, BLOCK), MASKED, jnp.float32)
+        )
+        top = jnp.max(peak, axis=1, keepdims=True)
+
+        def mix(c, total):
+            weights = jnp.exp2((scores[c] - top) * factor).astype(jnp.bfloat16)
+            values = vbuf[h, pl.ds(pl.multiple_of(c * CHUNK, CHUNK), CHUNK), :]
+            return total + jnp.dot(weights, values, preferred_element_type=jnp.float32)
+
+        total = lax.fori_loop(0, chunks, mix, jnp.zeros((rows, 2 * HD), jnp.float32))
+        result = (total[:, :HD] / total[:, HD:]).astype(jnp.bfloat16)
+        for j in range(group):
+            head = h * group + j
+            out_ref[part * span : (part + 1) * span, head * HD : (head + 1) * HD] = result[
+                j * span : (j + 1) * span
+            ]
 
 
 def attend_kernel(
@@ -71,39 +109,47 @@
 
         chunks = (count + 1) // 2
 
-        for h in range(KVH):
-            query = rot_ref[part, h * group : (h + 1) * group].reshape(rows, HD)
-
-            def score(c, peak):
-                keys = kbuf[h, pl.ds(pl.multiple_of(c * CHUNK, CHUNK), CHUNK), :]
-                s = lax.dot_general(
-                    query, keys, (((1,), (1,)), ((), ())), preferred_element_type=jnp.float32
-                )
-                col = c * CHUNK + lax.broadcasted_iota(jnp.int32, (span, CHUNK), 1)
-                line = offset + lax.broadcasted_iota(jnp.int32, (span, CHUNK), 0)
-                live = (col < count * BLOCK) & ((col >= BLOCK) | (col <= line))
-                bias = jnp.where(live, 0.0, MASKED)
-                s = (s.reshape(group, span, CHUNK) + bias[None]).reshape(rows, CHUNK)
-                scores[c] = s
-                return jnp.maximum(peak, jnp.maximum(s[:, :BLOCK], s[:, BLOCK:]))
-
-            peak = lax.fori_loop(
-                0, chunks, score, jnp.full((rows, BLOCK), MASKED, jnp.float32)
+        if scores.shape[0] > 4:
+            attend_long(
+                part, count, chunks, offset, span, group, rot_ref, kbuf, vbuf, scores, out_ref
             )
-            top = jnp.max(peak, axis=1, keepdims=True)
-
-            def mix(c, total):
-                weights = jnp.exp2((scores[c] - top) * factor).astype(jnp.bfloat16)
-                values = vbuf[h, pl.ds(pl.multiple_of(c * CHUNK, CHUNK), CHUNK), :]
-                return total + jnp.dot(weights, values, preferred_element_type=jnp.float32)
-
-            total = lax.fori_loop(0, chunks, mix, jnp.zeros((rows, 2 * HD), jnp.float32))
-            result = (total[:, :HD] / total[:, HD:]).astype(jnp.bfloat16)
-            for j in range(group):
-                head = h * group + j
-                out_ref[part * span : (part + 1) * span, head * HD : (head + 1) * HD] = result[
-                    j * span : (j + 1) * span
-                ]
+            continue
+
+        line = offset + lax.broadcasted_iota(jnp.int32, (span, BLOCK), 0)
+        col = lax.broadcasted_iota(jnp.int32, (span, BLOCK), 1)
+        first_bias = jnp.where(col <= line, 0.0, MASKED)[None]
+        last_bias = jnp.where(count % 2 == 1, MASKED, 0.0)
+
+        for v in range(1, scores.shape[0] + 1):
+
+            @pl.when(chunks == v)
+            def _(v=v):
+                def one_head(h, carry):
+                    query = rot_ref[part, pl.ds(h * group, group)].reshape(rows, HD)
+                    keys = kbuf[h, : v * CHUNK]
+                    s = lax.dot_general(
+                        query, keys, (((1,), (1,)), ((), ())), preferred_element_type=jnp.float32
+                    )
+                    front = s[:, :BLOCK].reshape(group, span, BLOCK) + first_bias
+                    pieces = [front.reshape(rows, BLOCK)]
+                    if v > 1:
+                        pieces.append(s[:, BLOCK:-BLOCK])
+                    pieces.append(s[:, -BLOCK:] + last_bias)
+                    s = jnp.concatenate(pieces, axis=1)
+                    top = jnp.max(s, axis=1, keepdims=True)
+                    weights = jnp.exp2((s - top) * factor).astype(jnp.bfloat16)
+                    total = jnp.dot(
+                        weights, vbuf[h, : v * CHUNK], preferred_element_type=jnp.float32
+                    )
+                    result = (total[:, :HD] / total[:, HD:]).astype(jnp.bfloat16)
+                    for j in range(group):
+                        to = pl.ds(pl.multiple_of((h * group + j) * HD, HD), HD)
+                        out_ref[part * span : (part + 1) * span, to] = result[
+                            j * span : (j + 1) * span
+                        ]
+                    return carry
+
+                lax.fori_loop(0, KVH, one_head, 0)
 
 
 def attend(n, pattern, span_pairs, rotated, kv, tok_rows):

time: 83.9 us -> 77.6 us (0.925)
  Pallas kernels: 79.3 us -> 72.7 us
    pallas_call x1, Pallas kernels: 17.8 us -> 11.2 us  [attend(): pl.pallas_call(functools.partial(attend_kernel, n), out_shape=jax.ShapeDt...]
where the time goes in v4:
time: 77.6 us; the launch traced here: 77.7 us
  Pallas kernels  72.7 us (94%)
  local copies, waits for them, and re-layouts  4.91 us (6%)
    pallas_call x1, Pallas kernels, project(): pl.pallas_call(functools.partial(project_kernel, n, groups), out_shape=(j...  61.5 us
    pallas_call x1, Pallas kernels, attend(): pl.pallas_call(functools.partial(attend_kernel, n), out_shape=jax.ShapeDt...  11.2 us
    unnamed x9, local copies, waits for them, and re-layouts  4.91 us

profile of v4, /device:TPU:1, one launch (start us, length us, event | category | flops | bytes accessed | tf_op | source)
XLA Modules:
  0.0 77.7 jit_solution(1969472143718977879)
XLA Ops:
  0.0 0.1 maximum_bitcast_fusion.frequency_ref
  0.1 0.8 copy.6.pattern_ref
  0.9 0.0 copy-start
  0.9 1.2 %copy-done = bf16[128,4096]{1,0:T(8,128)(2,1)S(1)} copy-done((bf16[128,4096]{1,0:T(8,128)(2,1)S(1)}, bf16[128,4096]{1,0:T(8,128)(2,1)}, u32[]{:S(2)}) %copy-start) | copy-done | bytes 1048600
  2.1 0.0 copy-start.1
  2.1 1.2 %copy-done.1 = bf16[128,4096]{1,0:T(8,128)(2,1)S(1)} copy-done((bf16[128,4096]{1,0:T(8,128)(2,1)S(1)}, bf16[128,4096]{1,0:T(8,128)(2,1)}, u32[]{:S(2)}) %copy-start.1) | copy-done | bytes 1048600
  3.3 0.0 copy-start.2
  3.3 1.0 %copy-done.2 = bf16[256,1024]{1,0:T(8,128)(2,1)S(1)} copy-done((bf16[256,1024]{1,0:T(8,128)(2,1)S(1)}, bf16[256,1024]{1,0:T(8,128)(2,1)}, u32[]{:S(2)}) %copy-start.2) | copy-done | bytes 524312
  4.3 0.0 copy-start.3
  4.4 0.7 copy-done.3
  5.0 61.5 %shard_map.55 = (bf16[2,32,64,128]{3,2,1,0:T(8,128)(2,1)S(1)}, bf16[2,16,128,512]{3,2,1,0:T(8,128)(2,1)S(1)}) custom-call(bf16[256,1024]{1,0:T(8,128)(2,1)S(1)} %copy-done.2, bf16[128,4096]{1,0:T(8,128)(2,1)S(1)} %copy-done, bf16[128,4096]{1,0:T(8,128)(2,1)S(1)} %copy-done.1, s32[16]{0:T(128)S(1)} %copy-done.3, f32[1,128]{1,0:T(1,128)S(1)} %maximum_bitcast_fusion.frequency_ref), custom_call_target="tpu_custom_call" | custom-call | tf_op jit(solution)/shard_map/pallas_call | solution.py:431
  66.5 11.2 %shard_map.56 = bf16[128,4096]{1,0:T(8,128)(2,1)} custom-call(s32[16,7]{1,0:T(8,128)S(1)} %copy.6.pattern_ref, s32[16]{0:T(128)S(1)} %copy-done.3, bf16[2,32,64,128]{3,2,1,0:T(8,128)(2,1)S(1)} %get-tuple-element.7.rot_ref, bf16[2,2048,512]{2,1,0:T(8,128)(2,1)S(1)} %bitcast.3), custom_call_target="tpu_custom_call" | custom-call | tf_op jit(solution)/shard_map/pallas_call | solution.py:162
  (1 shorter events, 0.0 us)
Async XLA Ops:
  0.9 1.2 %copy-start = (bf16[128,4096]{1,0:T(8,128)(2,1)S(1)}, bf16[128,4096]{1,0:T(8,128)(2,1)}, u32[]{:S(2)}) copy-start(bf16[128,4096]{1,0:T(8,128)(2,1)} %hidden_ref.1) | copy-start | bytes 3145732
  2.1 1.2 %copy-start.1 = (bf16[128,4096]{1,0:T(8,128)(2,1)S(1)}, bf16[128,4096]{1,0:T(8,128)(2,1)}, u32[]{:S(2)}) copy-start(bf16[128,4096]{1,0:T(8,128)(2,1)} %queries_ref.1) | copy-start | bytes 3145732
  3.3 1.0 %copy-start.2 = (bf16[256,1024]{1,0:T(8,128)(2,1)S(1)}, bf16[256,1024]{1,0:T(8,128)(2,1)}, u32[]{:S(2)}) copy-start(bf16[256,1024]{1,0:T(8,128)(2,1)} %weight_ref.1) | copy-start | bytes 1572868
  4.3 0.7 copy-start.3

commit v5 on v4

--- a/solution.py
+++ b/solution.py
@@ -428,6 +428,9 @@
     smem = pl.BlockSpec(memory_space=pltpu.SMEM)
     vmem = pl.BlockSpec(memory_space=pltpu.VMEM)
     dma = pltpu.SemaphoreType.DMA
+    weight, hidden, queries = (
+        pltpu.with_memory_space_constraint(x, pltpu.HBM) for x in (weight, hidden, queries)
+    )
     return pl.pallas_call(
         functools.partial(project_kernel, n, groups),
         out_shape=(

time: 77.6 us -> 74.2 us (0.956); the launches traced: 77.7 us -> 73.5 us
  local copies, waits for them, and re-layouts: 4.91 us -> 1.42 us
    unnamed x9 -> x3, local copies, waits for them, and re-layouts: 4.91 us -> 1.42 us
    pallas_call x1, Pallas kernels: 11.2 us -> 10.3 us  [attend(): pl.pallas_call(functools.partial(attend_kernel, n), out_shape=jax.ShapeDt...]
where the time goes in v5:
time: 74.2 us; the launch traced here: 73.5 us
  Pallas kernels  72 us (97%)
  local copies, waits for them, and re-layouts  1.42 us (2%)
    pallas_call x1, Pallas kernels, project(): pl.pallas_call(functools.partial(project_kernel, n, groups), out_shape=(j...  61.7 us
    pallas_call x1, Pallas kernels, attend(): pl.pallas_call(functools.partial(attend_kernel, n), out_shape=jax.ShapeDt...  10.3 us

profile of v5, /device:TPU:1, one launch (start us, length us, event | category | flops | bytes accessed | tf_op | source)
XLA Modules:
  0.0 73.5 jit_solution(3485245756752780567)
XLA Ops:
  0.0 0.1 maximum_bitcast_fusion.frequency_ref
  0.1 0.8 %copy.6.pattern_ref = s32[16,7]{1,0:T(8,128)S(1)} copy(s32[16,7]{0,1:T(8,128)} %param.8) | data formatting | bytes 896 | tf_op args[3]
  0.9 0.0 copy-start
  0.9 0.7 copy-done
  1.5 61.7 %shard_map.55 = (bf16[2,32,64,128]{3,2,1,0:T(8,128)(2,1)S(1)}, bf16[2,16,128,512]{3,2,1,0:T(8,128)(2,1)S(1)}) custom-call(bf16[256,1024]{1,0:T(8,128)(2,1)} %weight_ref.1, bf16[128,4096]{1,0:T(8,128)(2,1)} %hidden_ref.1, bf16[128,4096]{1,0:T(8,128)(2,1)} %queries_ref.1, s32[16]{0:T(128)S(1)} %copy-done, f32[1,128]{1,0:T(1,128)S(1)} %maximum_bitcast_fusion.frequency_ref), custom_call_target="tpu_custom_call" | custom-call | tf_op jit(solution)/shard_map/pallas_call | solution.py:434
  63.2 10.3 %shard_map.56 = bf16[128,4096]{1,0:T(8,128)(2,1)} custom-call(s32[16,7]{1,0:T(8,128)S(1)} %copy.6.pattern_ref, s32[16]{0:T(128)S(1)} %copy-done, bf16[2,32,64,128]{3,2,1,0:T(8,128)(2,1)S(1)} %get-tuple-element.7.rot_ref, bf16[2,2048,512]{2,1,0:T(8,128)(2,1)S(1)} %bitcast.3), custom_call_target="tpu_custom_call" | custom-call | tf_op jit(solution)/shard_map/pallas_call | solution.py:162
  (1 shorter events, 0.0 us)
Async XLA Ops:
  0.9 0.7 copy-start

commit v6 on v5

--- a/solution.py
+++ b/solution.py
@@ -175,7 +175,6 @@
 
 
 MESH = pl.DeviceIdType.MESH
-KBLOCK = 512
 
 
 def project_kernel(
@@ -355,17 +354,15 @@
             tables.at[source], tables.at[source], table_sems.at[0, d], table_sems.at[1, d], peers[d]
         ).wait_recv()
 
-    product[...] = jnp.zeros_like(product)
-
-    def multiply(k, carry):
-        at = pl.ds(pl.multiple_of(k * KBLOCK, KBLOCK), KBLOCK)
-        x = states[:, :, at].reshape(groups * tok_rows, KBLOCK)
-        product[...] += jnp.dot(
-            x, weights[at, :], preferred_element_type=jnp.float32
-        ).reshape(product.shape)
+    def multiply(c, carry):
+        at = pl.ds(pl.multiple_of(c * CHUNK, CHUNK), CHUNK)
+        x = states[...].reshape(groups * tok_rows, states.shape[2])
+        product[:, :, at] = jnp.dot(
+            x, weights[:, at], preferred_element_type=jnp.float32
+        ).reshape(groups, tok_rows, CHUNK)
         return carry
 
-    lax.fori_loop(0, states.shape[2] // KBLOCK, multiply, 0)
+    lax.fori_loop(0, width // CHUNK, multiply, 0)
 
     is_key = g * width < KVH * HD
 

time: 74.2 us -> 74.1 us (level)
    pallas_call x1, Pallas kernels: 10.3 us -> 11.7 us  [attend(): pl.pallas_call(functools.partial(attend_kernel, n), out_shape=jax.ShapeDt...]
    pallas_call x1, Pallas kernels: 61.7 us -> 60.7 us  [project(): pl.pallas_call(functools.partial(project_kernel, n, groups), out_shape=(j...]
where the time goes in v6:
time: 74.1 us; the launch traced here: 73.9 us
  Pallas kernels  72.4 us (98%)
  local copies, waits for them, and re-layouts  1.42 us (2%)
    pallas_call x1, Pallas kernels, project(): pl.pallas_call(functools.partial(project_kernel, n, groups), out_shape=(j...  60.7 us
    pallas_call x1, Pallas kernels, attend(): pl.pallas_call(functools.partial(attend_kernel, n), out_shape=jax.ShapeDt...  11.7 us

profile of v6, /device:TPU:1, one launch (start us, length us, event | category | flops | bytes accessed | tf_op | source)
XLA Modules:
  0.0 73.9 jit_solution(6993608654838671644)
XLA Ops:
  0.0 0.1 maximum_bitcast_fusion.frequency_ref
  0.1 0.8 %copy.6.pattern_ref = s32[16,7]{1,0:T(8,128)S(1)} copy(s32[16,7]{0,1:T(8,128)} %param.8) | data formatting | bytes 896 | tf_op args[3]
  0.9 0.0 copy-start
  0.9 0.7 copy-done
  1.5 60.7 %shard_map.55 = (bf16[2,32,64,128]{3,2,1,0:T(8,128)(2,1)S(1)}, bf16[2,16,128,512]{3,2,1,0:T(8,128)(2,1)S(1)}) custom-call(bf16[256,1024]{1,0:T(8,128)(2,1)} %weight_ref.1, bf16[128,4096]{1,0:T(8,128)(2,1)} %hidden_ref.1, bf16[128,4096]{1,0:T(8,128)(2,1)} %queries_ref.1, s32[16]{0:T(128)S(1)} %copy-done, f32[1,128]{1,0:T(1,128)S(1)} %maximum_bitcast_fusion.frequency_ref), custom_call_target="tpu_custom_call" | custom-call | tf_op jit(solution)/shard_map/pallas_call | solution.py:431
  62.2 11.7 %shard_map.56 = bf16[128,4096]{1,0:T(8,128)(2,1)} custom-call(s32[16,7]{1,0:T(8,128)S(1)} %copy.6.pattern_ref, s32[16]{0:T(128)S(1)} %copy-done, bf16[2,32,64,128]{3,2,1,0:T(8,128)(2,1)S(1)} %get-tuple-element.7.rot_ref, bf16[2,2048,512]{2,1,0:T(8,128)(2,1)S(1)} %bitcast.3), custom_call_target="tpu_custom_call" | custom-call | tf_op jit(solution)/shard_map/pallas_call | solution.py:162
  (1 shorter events, 0.0 us)
Async XLA Ops:
  0.9 0.7 copy-start

commit v7 on v6

--- a/solution.py
+++ b/solution.py
@@ -149,7 +149,7 @@
                         ]
                     return carry
 
-                lax.fori_loop(0, KVH, one_head, 0)
+                lax.fori_loop(0, KVH, one_head, 0, unroll=2)
 
 
 def attend(n, pattern, span_pairs, rotated, kv, tok_rows):

time: 74.1 us -> 71.5 us (0.965)
  Pallas kernels: 72.4 us -> 69.8 us
    pallas_call x1, Pallas kernels: 11.7 us -> 9.08 us  [attend(): pl.pallas_call(functools.partial(attend_kernel, n), out_shape=jax.ShapeDt...]
where the time goes in v7:
time: 71.5 us; the launch traced here: 71.3 us
  Pallas kernels  69.8 us (98%)
  local copies, waits for them, and re-layouts  1.42 us (2%)
    pallas_call x1, Pallas kernels, project(): pl.pallas_call(functools.partial(project_kernel, n, groups), out_shape=(j...  60.7 us
    pallas_call x1, Pallas kernels, attend(): pl.pallas_call(functools.partial(attend_kernel, n), out_shape=jax.ShapeDt...  9.08 us

profile of v7, /device:TPU:1, one launch (start us, length us, event | category | flops | bytes accessed | tf_op | source)
XLA Modules:
  0.0 71.3 jit_solution(16797112139614712683)
XLA Ops:
  0.0 0.1 maximum_bitcast_fusion.frequency_ref
  0.1 0.8 %copy.6.pattern_ref = s32[16,7]{1,0:T(8,128)S(1)} copy(s32[16,7]{0,1:T(8,128)} %param.8) | data formatting | bytes 896 | tf_op args[3]
  0.9 0.0 copy-start
  0.9 0.7 copy-done
  1.5 60.7 %shard_map.55 = (bf16[2,32,64,128]{3,2,1,0:T(8,128)(2,1)S(1)}, bf16[2,16,128,512]{3,2,1,0:T(8,128)(2,1)S(1)}) custom-call(bf16[256,1024]{1,0:T(8,128)(2,1)} %weight_ref.1, bf16[128,4096]{1,0:T(8,128)(2,1)} %hidden_ref.1, bf16[128,4096]{1,0:T(8,128)(2,1)} %queries_ref.1, s32[16]{0:T(128)S(1)} %copy-done, f32[1,128]{1,0:T(1,128)S(1)} %maximum_bitcast_fusion.frequency_ref), custom_call_target="tpu_custom_call" | custom-call | tf_op jit(solution)/shard_map/pallas_call | solution.py:431
  62.2 9.1 %shard_map.56 = bf16[128,4096]{1,0:T(8,128)(2,1)} custom-call(s32[16,7]{1,0:T(8,128)S(1)} %copy.6.pattern_ref, s32[16]{0:T(128)S(1)} %copy-done, bf16[2,32,64,128]{3,2,1,0:T(8,128)(2,1)S(1)} %get-tuple-element.7.rot_ref, bf16[2,2048,512]{2,1,0:T(8,128)(2,1)S(1)} %bitcast.3), custom_call_target="tpu_custom_call" | custom-call | tf_op jit(solution)/shard_map/pallas_call | solution.py:162
  (1 shorter events, 0.0 us)
Async XLA Ops:
  0.9 0.7 copy-start
